TPU v7x, 32 devices: a whole 2x2x4 slice. The times are simulated.
32 devices in a mesh: rows: 8 (over y, x, core), cols: 4 (over z).
Axes of the slice: x: 2, y: 2, z: 4, core: 2. Of those that a mesh axis runs over, the one named last changes fastest.
Arguments:
- block_input: bfloat16 [256, 256, 512], P('rows', 'cols'), may hold values from -18 to 18
- norm_gain: bfloat16 [512], replicated, may hold values from 0.5 to 1.5
- saved_queries: bfloat16 [256, 256, 512], P('rows', 'cols'), may hold values from -8 to 8
- saved_keys: bfloat16 [256, 256, 512], P('rows', 'cols'), may hold values from -8 to 8
- saved_values: bfloat16 [256, 256, 512], P('rows', 'cols'), may hold values from -6 to 6
- out_grad: bfloat16 [256, 256, 512], P('rows', 'cols'), may hold values from -6 to 6
- w_query: bfloat16 [512, 512], replicated, may hold values from -0.25 to 0.25
- w_key: bfloat16 [512, 512], replicated, may hold values from -0.25 to 0.25
- w_value: bfloat16 [512, 512], replicated, may hold values from -0.25 to 0.25
- w_out: bfloat16 [512, 512], replicated, may hold values from -0.25 to 0.25
Outputs:
- block_grad: float32 [256, 256, 512], P('rows', 'cols')
All inputs are finite; a program needn't handle non-finite values.
Results may differ from a plain program's by a relative error of at most 0.0044.
Values may be sent and summed in bfloat16 or wider, within the bound.
A program may use at most 128 MiB of HBM per device.

v0:
```python
import jax
import jax.numpy as jnp
from jax import lax
from jax.sharding import PartitionSpec as P

D = 512
HEADS = 16
GRID = 16


def window_grads(items):
    query_win, key_win, value_win, grad_win = items
    length = query_win.shape[0]
    head_dim = D // HEADS
    factor = head_dim ** (-0.5)
    query_heads = query_win.reshape(length, HEADS, head_dim)
    key_heads = key_win.reshape(length, HEADS, head_dim)
    value_heads = value_win.reshape(length, HEADS, head_dim)
    grad_heads = grad_win.reshape(length, HEADS, head_dim)
    scores = (
        jnp.einsum("qhd,khd->hqk", query_heads, key_heads, preferred_element_type=jnp.float32)
        * factor
    )
    attention = jax.nn.softmax(scores, axis=-1)
    value_grad = jnp.einsum(
        "hqk,qhd->khd",
        attention.astype(jnp.bfloat16),
        grad_heads,
        preferred_element_type=jnp.float32,
    ).astype(jnp.bfloat16)
    prob_grad = jnp.einsum(
        "qhd,khd->hqk", grad_heads, value_heads, preferred_element_type=jnp.float32
    )
    centre = jnp.sum(attention * prob_grad, axis=-1, keepdims=True)
    score_grad = (attention * (prob_grad - centre)).astype(jnp.bfloat16)
    query_grad = (
        jnp.einsum("hqk,khd->qhd", score_grad, key_heads, preferred_element_type=jnp.float32)
        * factor
    ).astype(jnp.bfloat16)
    key_grad = (
        jnp.einsum("hqk,qhd->khd", score_grad, query_heads, preferred_element_type=jnp.float32)
        * factor
    ).astype(jnp.bfloat16)
    return (
        query_grad.reshape(length, D),
        key_grad.reshape(length, D),
        value_grad.reshape(length, D),
    )


def transposed_product(left, weight):
    return lax.dot_general(
        left, weight, (((1,), (1,)), ((), ())), preferred_element_type=jnp.float32
    )


def project_back(query_grad, key_grad, value_grad, w_query, w_key, w_value):
    total = transposed_product(query_grad, w_query) + transposed_product(key_grad, w_key)
    return (total + transposed_product(value_grad, w_value)).astype(jnp.bfloat16)


def norm_backward(block_input, norm_gain, input_grad):
    values_in = block_input.astype(jnp.float32)
    centred = values_in - jnp.mean(values_in, axis=-1, keepdims=True)
    variance = jnp.mean(centred * centred, axis=-1, keepdims=True)
    inv_std = lax.rsqrt(variance + 1e-05)
    normed = centred * inv_std
    scaled = input_grad.astype(jnp.float32) * norm_gain.astype(jnp.float32)
    return inv_std * (
        scaled
        - jnp.mean(scaled, axis=-1, keepdims=True)
        - normed * jnp.mean(scaled * normed, axis=-1, keepdims=True)
    )


def on_device(
    block_input,
    norm_gain,
    saved_queries,
    saved_keys,
    saved_values,
    out_grad,
    w_query,
    w_key,
    w_value,
    w_out,
):
    rows_dev = block_input.shape[0]
    cols_dev = block_input.shape[1]
    row_count = lax.axis_size("rows")
    col_count = lax.axis_size("cols")
    row_stride = rows_dev * row_count // GRID
    col_stride = cols_dev * col_count // GRID
    row_reps = rows_dev // row_stride
    col_reps = cols_dev // col_stride
    row_part = row_stride // row_count
    col_part = col_stride // col_count
    windows = row_part * col_part
    length = GRID * GRID
    tokens_dev = rows_dev * cols_dev
    flat_grad = out_grad.reshape(tokens_dev, D)
    out_proj_grad = (
        transposed_product(flat_grad, w_out).astype(jnp.bfloat16).reshape(rows_dev, cols_dev, D)
    )
    packed = jnp.stack((saved_queries, saved_keys, saved_values, out_proj_grad))
    spread = packed.reshape(4, row_reps, row_stride, col_reps, col_stride, D).transpose(
        0, 2, 4, 1, 3, 5
    )
    arrived = lax.all_to_all(
        lax.all_to_all(spread, "rows", split_axis=1, concat_axis=3, tiled=True),
        "cols",
        split_axis=2,
        concat_axis=4,
        tiled=True,
    )
    grouped = arrived.reshape(4, windows, length, D)
    query_grad, key_grad, value_grad = lax.map(
        window_grads, (grouped[0], grouped[1], grouped[2], grouped[3])
    )
    back_in = jnp.stack((query_grad, key_grad, value_grad))
    members = back_in.shape[0]
    sectioned = back_in.reshape(members, row_part, col_part, GRID, GRID, D)
    returned = lax.all_to_all(
        lax.all_to_all(sectioned, "rows", split_axis=3, concat_axis=1, tiled=True),
        "cols",
        split_axis=4,
        concat_axis=2,
        tiled=True,
    )
    tile_view = returned.transpose(0, 3, 1, 4, 2, 5).reshape(members, tokens_dev, D)
    input_grad = project_back(tile_view[0], tile_view[1], tile_view[2], w_query, w_key, w_value)
    branch = norm_backward(block_input.reshape(tokens_dev, D), norm_gain, input_grad)
    return (flat_grad.astype(jnp.float32) + branch).reshape(rows_dev, cols_dev, D)


def solution(mesh):
    return jax.shard_map(
        on_device,
        mesh=mesh,
        in_specs=(
            P("rows", "cols", None),
            P(),
            P("rows", "cols", None),
            P("rows", "cols", None),
            P("rows", "cols", None),
            P("rows", "cols", None),
            P(),
            P(),
            P(),
            P(),
        ),
        out_specs=P("rows", "cols", None),
        check_vma=False,
    )
```

profile of v0, /device:TPU:0, one launch (start us, length us, event | category | flops | bytes accessed | tf_op | source)
XLA Modules:
  0.0 778.2 jit_solution(6522818777771074800)
XLA Ops:
  3.7 3.8 maximum_bitcast_fusion
  7.5 8.5 %copy.105 = bf16[4,16,16,2,4,512]{5,2,4,3,0,1:T(8,128)(2,1)} copy(bf16[4,16,16,2,4,512]{5,2,4,1,3,0:T(8,128)(2,1)} %maximum_bitcast_fusion) | data formatting | bytes 16777216 | tf_op jit(solution)/shard_map/transpose | solution.py:106
  16.0 100.4 %all_to_all.69 = bf16[4,16,16,2,4,512]{5,2,4,3,0,1:T(8,128)(2,1)} all-to-all(bf16[4,16,16,2,4,512]{5,2,4,3,0,1:T(8,128)(2,1)} %copy.105), channel_id=1, replica_groups=mesh['rows'=8,'cols'=4] {'rows'}, dimensions={1} | all-to-all | bytes 16777216 | tf_op jit(solution)/shard_map/all_to_all | solution.py:110
  116.4 8.5 %copy.107 = bf16[4,2,16,8,2,4,512]{6,2,5,4,3,1,0:T(8,128)(2,1)} copy(bf16[4,2,16,8,2,4,512]{6,2,5,4,0,1,3:T(8,128)(2,1)} %bitcast.105) | data formatting | bytes 16777216 | tf_op jit(solution)/shard_map/all_to_all | solution.py:110
  124.9 9.5 %copy.108 = bf16[4,2,16,16,4,512]{5,4,3,1,0,2:T(4,128)(2,1)} copy(bf16[4,2,16,16,4,512]{5,2,4,3,1,0:T(8,128)(2,1)} %bitcast.106) | data formatting | bytes 16777216 | tf_op jit(solution)/shard_map/all_to_all | solution.py:110
  134.3 5.9 all-to-all-start.1
  140.2 183.4 %all-to-all-done.1 = bf16[4,2,16,16,4,512]{5,4,3,1,0,2:T(4,128)(2,1)} async-done(((bf16[4,2,16,16,4,512]{5,4,3,1,0,2:T(4,128)(2,1)}), bf16[4,2,16,16,4,512]{5,4,3,1,0,2:T(4,128)(2,1)}, u32[]{:S(2)}, u32[]{:S(2)}) %all-to-all-start.1) | async-done | bytes 8388640 | tf_op jit(solution)/shard_map/all_to_all | solution.py:109
  323.6 9.6 %copy.109 = bf16[4,2,16,16,4,512]{5,3,4,2,1,0:T(8,128)(2,1)} copy(bf16[4,2,16,16,4,512]{5,4,3,1,0,2:T(4,128)(2,1)} %all-to-all-done.1) | data formatting | bytes 16777216 | tf_op jit(solution)/shard_map/all_to_all | solution.py:109
  333.2 5.8 fusion.18
  358.6 162.9 %while.14 = (s32[]{:T(128)}, bf16[8,256,512]{2,1,0:T(8,128)(2,1)}, bf16[8,256,512]{2,1,0:T(8,128)(2,1)}, bf16[8,256,512]{2,1,0:T(8,128)(2,1)}, bf16[8,256,512]{2...) while((s32[]{:T(128)}, bf16[8,256,512]{2,1,0:T(8,128)(2,1)}, ...), condition=%wide.region_6.7_spmd, body=%wide.region_2.6_spmd.sunk | while | flops 348778752 | bytes 59344036 | solution.py:117
  372.1 3.7 fusion.67
  392.4 3.7 fusion.67
  412.7 3.7 fusion.67
  433.1 3.7 fusion.67
  442.3 3.5 fusion.65
  453.4 3.7 fusion.67
  473.8 3.7 fusion.67
  494.1 3.7 fusion.67
  514.5 3.7 fusion.67
  526.0 74.1 %all_to_all.70 = bf16[3,2,4,16,16,512]{5,4,2,1,0,3:T(8,128)(2,1)S(1)} all-to-all(bf16[3,2,4,16,16,512]{5,4,2,1,0,3:T(8,128)(2,1)S(1)} %copy.121), channel_id=1, replica_groups=mesh['rows'=8,'cols'=4] {'rows'}, dimensions={3} | all-to-all | bytes 12582912 | tf_op jit(solution)/shard_map/all_to_all | solution.py:124
  601.1 13.9 %copy.124 = bf16[3,16,4,2,16,512]{5,3,2,1,0,4:T(2,128)(2,1)} copy(bf16[3,16,4,2,16,512]{5,4,3,2,1,0:T(8,128)(2,1)S(1)} %bitcast.115) | data formatting | bytes 12582912 | tf_op jit(solution)/shard_map/all_to_all | solution.py:124
  615.0 5.6 all-to-all-start.3
  622.1 136.3 %all-to-all-done.3 = bf16[3,16,4,2,16,512]{5,3,2,1,0,4:T(2,128)(2,1)} async-done(((bf16[3,16,4,2,16,512]{5,3,2,1,0,4:T(2,128)(2,1)}), bf16[3,16,4,2,16,512]{5,3,2,1,0,4:T(2,128)(2,1)}, u32[]{:S(2)}, u32[]{:S(2)}) %all-to-all-start.3) | async-done | bytes 6291488 | tf_op jit(solution)/shard_map/all_to_all | solution.py:123
  758.4 5.0 copy.125
  (225 shorter events, 173.0 us)
Async XLA Ops:
  0.0 771.7 %copy-start = (bf16[512,512]{1,0:T(8,128)(2,1)S(1)}, bf16[512,512]{1,0:T(8,128)(2,1)}, u32[]{:S(2)}) copy-start(bf16[512,512]{1,0:T(8,128)(2,1)} %param.20) | copy-start | bytes 1572868
  0.0 3.1 copy-start.5
  0.0 3.1 copy-start.6
  0.0 3.7 copy-start.7
  134.3 189.3 %all-to-all-start.1 = ((bf16[4,2,16,16,4,512]{5,4,3,1,0,2:T(4,128)(2,1)}), bf16[4,2,16,16,4,512]{5,4,3,1,0,2:T(4,128)(2,1)}, u32[]{:S(2)}, u32[]{:S(2)}) async-start(bf16[4,2,16,16,4,512]{5,4,3,1,0,2:T(4,128)(2,1)} %copy.108), calls=%async_computation.1 | async-start | bytes 16777216 | tf_op jit(solution)/shard_map/all_to_all | solution.py:109
  365.6 4.4 copy-start.3
  366.9 3.5 copy-start.1
  385.9 4.4 copy-start.3
  387.2 3.5 copy-start.1
  406.3 4.4 copy-start.3
  407.5 3.5 copy-start.1
  426.6 4.4 copy-start.3
  427.8 3.5 copy-start.1
  447.0 4.4 copy-start.3
  448.2 3.5 copy-start.1
  467.3 4.4 copy-start.3
  468.6 3.5 copy-start.1
  487.7 4.4 copy-start.3
  488.9 3.5 copy-start.1
  508.0 4.4 copy-start.3
  509.2 3.5 copy-start.1
  615.0 5.7 copy-start.2
  615.0 143.4 %all-to-all-start.3 = ((bf16[3,16,4,2,16,512]{5,3,2,1,0,4:T(2,128)(2,1)}), bf16[3,16,4,2,16,512]{5,3,2,1,0,4:T(2,128)(2,1)}, u32[]{:S(2)}, u32[]{:S(2)}) async-start(bf16[3,16,4,2,16,512]{5,3,2,1,0,4:T(2,128)(2,1)} %copy.124), calls=%async_computation.3 | async-start | bytes 12582912 | tf_op jit(solution)/shard_map/all_to_all | solution.py:123
  771.7 2.5 copy-start.4
  (3 other events, 5.1 us)
where the time goes:
time: 784 us; the launch traced here: 778 us
  waiting for transfers between devices  320 us (41%)
  blocking collectives  174 us (22%)
  local copies, waits for them, and re-layouts  151 us (19%)
  matrix products  101 us (13%)
  other arithmetic  19.3 us (2%)
  starting transfers between devices  11.5 us (1%)
    all_to_all x1, waiting for transfers between devices, on_device(): lax.all_to_all(lax.all_to_all(spread, 'rows', split_axis=1, concat_axis=3...  183 us
    all_to_all x1, waiting for transfers between devices, on_device(): lax.all_to_all(lax.all_to_all(sectioned, 'rows', split_axis=3, concat_axi...  136 us
    all_to_all x1, blocking collectives, on_device(): lax.all_to_all(spread, 'rows', split_axis=1, concat_axis=3, tiled=True)  100 us
    all_to_all x1, blocking collectives, on_device(): lax.all_to_all(sectioned, 'rows', split_axis=3, concat_axis=1, tiled=True)  74.1 us
    dynamic_slice x64, local copies, waits for them, and re-layouts, on_device(): lax.map(window_grads, (grouped[0], grouped[1], grouped[2], grouped[3]))  36.1 us
    dot_general x8, matrix products, window_grads(): jnp.einsum('hqk,qhd->khd', attention.astype(jnp.bfloat16), grad_heads, pr...  29.8 us
    sub x8, matrix products, window_grads(): attention = jax.nn.softmax(scores, axis=-1)  28.3 us
    dot_general x8, matrix products, window_grads(): jnp.einsum('qhd,khd->hqk', grad_heads, value_heads, preferred_element_typ...  25.1 us
  transfers between devices with their start and end apart: 2, of which 2 were waited for; matrix products, arithmetic and copies ran while one was open for 0% of the time, Pallas kernels for 0%

commit v1 on v0

v1 whole, which is shorter than its diff:
```python
import functools

import jax
import jax.numpy as jnp
import numpy as np
from jax import lax
from jax.experimental import pallas as pl
from jax.experimental.pallas import tpu as pltpu
from jax.sharding import PartitionSpec as P

D = 512
HEADS = 16
GRID = 16
HEAD_DIM = D // HEADS
LANES = 128
LENGTH = GRID * GRID
FACTOR = HEAD_DIM ** (-0.5)
EXP2_FACTOR = FACTOR * float(np.log2(np.e))
MESH = pl.DeviceIdType.MESH
VMEM_BYTES = 50 * 1024 * 1024
F32 = jnp.float32
BF16 = jnp.bfloat16


def dot(left, right):
    return lax.dot_general(left, right, (((1,), (0,)), ((), ())), preferred_element_type=F32)


def dot_t(left, right):
    return lax.dot_general(left, right, (((1,), (1,)), ((), ())), preferred_element_type=F32)


def pack_kernel(perm_ref, w_out_ref, q_ref, k_ref, v_ref, g_ref, out_ref):
    chunks, _, cols, _, rows, _ = out_ref.shape
    perm = perm_ref[...]
    tokens = perm.shape[0]
    for member, ref in enumerate((q_ref, k_ref, v_ref, g_ref)):
        ordered = dot(perm, ref[...].reshape(tokens, D)).astype(BF16)
        if member == 3:
            ordered = dot_t(ordered, w_out_ref[...]).astype(BF16)
        out_ref[:, 0, :, member] = ordered.reshape(chunks, cols, rows, D)


def norm_kernel(perm_ref, gain_ref, x_ref, g_ref, back_ref, out_ref):
    perm = perm_ref[...]
    tokens = perm.shape[0]
    input_grad = dot(perm, back_ref[...].reshape(tokens, D))
    values_in = x_ref[...].reshape(tokens, D).astype(F32)
    centred = values_in - jnp.mean(values_in, axis=-1, keepdims=True)
    variance = jnp.mean(centred * centred, axis=-1, keepdims=True)
    inv_std = lax.rsqrt(variance + 1e-05)
    normed = centred * inv_std
    scaled = input_grad * gain_ref[...].astype(F32)
    branch = inv_std * (
        scaled
        - jnp.mean(scaled, axis=-1, keepdims=True)
        - normed * jnp.mean(scaled * normed, axis=-1, keepdims=True)
    )
    out_ref[...] = (g_ref[...].reshape(tokens, D).astype(F32) + branch).reshape(out_ref.shape)


def window_kernel(
    row_count, col_count, wins, part,
    send_ref, w_query_ref, w_key_ref, w_value_ref, back_ref,
    recv, reply, q_win, k_win, v_win, g_win, k_turned, dq_turned, dk_win, dv_win,
    send_sem, recv_sem, reply_sem, back_sem,
):
    chunks, devices, _, rows, _ = send_ref.shape
    my_row, my_col = lax.axis_index("rows"), lax.axis_index("cols")
    me = my_row * col_count + my_col

    def peer_of(step):
        row = lax.rem(my_row + step // col_count, row_count)
        col = lax.rem(my_col + lax.rem(step, col_count), col_count)
        return row, col, row * col_count + col

    barrier = pltpu.get_barrier_semaphore()

    @pl.loop(1, devices)
    def _(step):
        row, col, _ = peer_of(step)
        pl.semaphore_signal(barrier, inc=1, device_id=(row, col), device_id_type=MESH)

    pl.semaphore_wait(barrier, devices - 1)

    @pl.loop(0, chunks)
    def _(chunk):
        pltpu.make_async_copy(
            send_ref.at[chunk, me], recv.at[chunk, me], recv_sem.at[chunk]
        ).start()

        @pl.loop(1, devices)
        def _(step):
            row, col, index = peer_of(step)
            pltpu.make_async_remote_copy(
                src_ref=send_ref.at[chunk, index],
                dst_ref=recv.at[chunk, me],
                send_sem=send_sem.at[chunk],
                recv_sem=recv_sem.at[chunk],
                device_id=(row, col),
                device_id_type=MESH,
            ).start()

    lane_head = lax.broadcasted_iota(jnp.int32, (1, LANES), 1) // HEAD_DIM
    spread = devices * rows

    @pl.loop(0, chunks)
    def _(chunk):
        pltpu.make_async_copy(recv.at[chunk], recv.at[chunk], recv_sem.at[chunk]).wait()
        reply[chunk] = jnp.zeros((devices, rows, D), BF16)

        @pl.loop(0, wins)
        def _(win):
            slot = lax.broadcasted_iota(jnp.int32, (LENGTH, spread), 0)
            place = lax.broadcasted_iota(jnp.int32, (LENGTH, spread), 1)
            pick = (place == (slot // part) * rows + win * part + slot % part).astype(BF16)
            for member, ref in enumerate((q_win, k_win, v_win, g_win)):
                ref[...] = dot(pick, recv[chunk, :, member].reshape(spread, D)).astype(BF16)
            k_turned[...] = k_win[...].astype(F32).T.astype(BF16)

            @pl.loop(0, D // LANES)
            def _(group):
                lanes = pl.ds(pl.multiple_of(group * LANES, LANES), LANES)
                q_part, k_part = q_win[:, lanes], k_win[:, lanes]
                v_part, g_part = v_win[:, lanes], g_win[:, lanes]
                value_grad = jnp.zeros((LENGTH, LANES), F32)
                key_grad = jnp.zeros((LENGTH, LANES), F32)
                for head in range(LANES // HEAD_DIM):
                    mask = (lane_head == head).astype(BF16)
                    q_head, g_head = q_part * mask, g_part * mask
                    scores = dot_t(k_part, q_head)
                    top = jnp.max(scores, axis=0, keepdims=True)
                    weights = jnp.exp2((scores - top) * EXP2_FACTOR)
                    attention = weights * (1.0 / jnp.sum(weights, axis=0, keepdims=True))
                    value_grad += dot(attention.astype(BF16), g_head)
                    prob_grad = dot_t(v_part, g_head)
                    centre = jnp.sum(attention * prob_grad, axis=0, keepdims=True)
                    score_grad = (attention * (prob_grad - centre)).astype(BF16)
                    key_grad += dot(score_grad, q_head)
                    dims = pl.ds(pl.multiple_of(group * LANES + head * HEAD_DIM, HEAD_DIM), HEAD_DIM)
                    dq_turned[dims, :] = dot(k_turned[dims, :], score_grad) * FACTOR
                dv_win[:, lanes] = value_grad.astype(BF16)
                dk_win[:, lanes] = (key_grad * FACTOR).astype(BF16)

            total = dot_t(dq_turned[...].T.astype(BF16), w_query_ref[...])
            total += dot_t(dk_win[...], w_key_ref[...])
            total += dot_t(dv_win[...], w_value_ref[...])
            place_t = lax.broadcasted_iota(jnp.int32, (spread, LENGTH), 0)
            slot_t = lax.broadcasted_iota(jnp.int32, (spread, LENGTH), 1)
            put = (place_t == (slot_t // part) * rows + win * part + slot_t % part).astype(BF16)
            placed = dot(put, total.astype(BF16)).astype(BF16)
            reply[chunk] += placed.reshape(devices, rows, D)

        pltpu.make_async_copy(
            reply.at[chunk, me], back_ref.at[chunk, me], back_sem.at[chunk]
        ).start()

        @pl.loop(1, devices)
        def _(step):
            row, col, index = peer_of(step)
            pltpu.make_async_remote_copy(
                src_ref=reply.at[chunk, index],
                dst_ref=back_ref.at[chunk, me],
                send_sem=reply_sem.at[chunk],
                recv_sem=back_sem.at[chunk],
                device_id=(row, col),
                device_id_type=MESH,
            ).start()

    @pl.loop(0, chunks)
    def _(chunk):
        sent = send_ref.at[chunk, pl.ds(0, devices - 1)]
        pltpu.make_async_copy(sent, sent, send_sem.at[chunk]).wait()
        replied = reply.at[chunk, pl.ds(0, devices - 1)]
        pltpu.make_async_copy(replied, replied, reply_sem.at[chunk]).wait()
        pltpu.make_async_copy(back_ref.at[chunk], back_ref.at[chunk], back_sem.at[chunk]).wait()


def on_device(
    block_input,
    norm_gain,
    saved_queries,
    saved_keys,
    saved_values,
    out_grad,
    w_query,
    w_key,
    w_value,
    w_out,
):
    rows_dev, cols_dev = block_input.shape[:2]
    row_count, col_count = lax.axis_size("rows"), lax.axis_size("cols")
    devices = row_count * col_count
    row_stride = rows_dev * row_count // GRID
    col_stride = cols_dev * col_count // GRID
    row_reps, col_reps = rows_dev // row_stride, cols_dev // col_stride
    row_part, col_part = row_stride // row_count, col_stride // col_count
    windows = row_part * col_part
    part = row_reps * col_reps
    wins = next(n for n in range(1, windows + 1) if windows % n == 0 and n * part % 16 == 0)
    chunks, rows = windows // wins, wins * part

    tokens = row_reps * row_part * cols_dev
    order = (
        np.arange(tokens)
        .reshape(row_reps, row_part, col_reps, col_count, col_part)
        .transpose(1, 4, 3, 0, 2)
        .reshape(chunks, wins, col_count, part)
        .transpose(0, 2, 1, 3)
        .reshape(tokens)
    )
    perm = np.zeros((tokens, tokens), np.float32)
    perm[np.arange(tokens), order] = 1.0
    forward, backward = jnp.asarray(perm, BF16), jnp.asarray(perm.T, BF16)

    def blocks(array):
        return array.reshape(row_reps, row_stride, cols_dev, D)

    token_spec = pl.BlockSpec((row_reps, row_part, cols_dev, D), lambda r: (0, r, 0, 0))
    perm_spec = pl.BlockSpec((tokens, tokens), lambda r: (0, 0))
    weight_spec = pl.BlockSpec((D, D), lambda r: (0, 0))
    params = pltpu.CompilerParams(vmem_limit_bytes=VMEM_BYTES)

    packed = pl.pallas_call(
        pack_kernel,
        grid=(row_count,),
        in_specs=[perm_spec, weight_spec] + [token_spec] * 4,
        out_specs=pl.BlockSpec(
            (chunks, 1, col_count, 4, rows, D), lambda r: (0, r, 0, 0, 0, 0)
        ),
        out_shape=jax.ShapeDtypeStruct((chunks, row_count, col_count, 4, rows, D), BF16),
        compiler_params=params,
    )(forward, w_out, blocks(saved_queries), blocks(saved_keys), blocks(saved_values), blocks(out_grad))

    vmem = pl.BlockSpec(memory_space=pltpu.VMEM)
    hbm = pl.BlockSpec(memory_space=pl.ANY)
    window = pltpu.VMEM((LENGTH, D), BF16)
    back = pl.pallas_call(
        functools.partial(window_kernel, row_count, col_count, wins, part),
        in_specs=[hbm, vmem, vmem, vmem],
        out_specs=hbm,
        out_shape=jax.ShapeDtypeStruct((chunks, devices, rows, D), BF16),
        scratch_shapes=[
            pltpu.VMEM((chunks, devices, 4, rows, D), BF16),
            pltpu.VMEM((chunks, devices, rows, D), BF16),
            window,
            window,
            window,
            window,
            pltpu.VMEM((D, LENGTH), BF16),
            pltpu.VMEM((D, LENGTH), F32),
            window,
            window,
            pltpu.SemaphoreType.DMA((chunks,)),
            pltpu.SemaphoreType.DMA((chunks,)),
            pltpu.SemaphoreType.DMA((chunks,)),
            pltpu.SemaphoreType.DMA((chunks,)),
        ],
        compiler_params=pltpu.CompilerParams(
            collective_id=0, has_side_effects=True, vmem_limit_bytes=VMEM_BYTES
        ),
    )(packed.reshape(chunks, devices, 4, rows, D), w_query, w_key, w_value)

    result = pl.pallas_call(
        norm_kernel,
        grid=(row_count,),
        in_specs=[
            perm_spec,
            pl.BlockSpec((1, D), lambda r: (0, 0)),
            token_spec,
            token_spec,
            pl.BlockSpec((chunks, 1, col_count, rows, D), lambda r: (0, r, 0, 0, 0)),
        ],
        out_specs=token_spec,
        out_shape=jax.ShapeDtypeStruct((row_reps, row_stride, cols_dev, D), F32),
        compiler_params=params,
    )(
        backward,
        norm_gain.reshape(1, D),
        blocks(block_input),
        blocks(out_grad),
        back.reshape(chunks, row_count, col_count, rows, D),
    )
    return result.reshape(rows_dev, cols_dev, D)


def solution(mesh):
    return jax.shard_map(
        on_device,
        mesh=mesh,
        in_specs=(
            P("rows", "cols", None),
            P(),
            P("rows", "cols", None),
            P("rows", "cols", None),
            P("rows", "cols", None),
            P("rows", "cols", None),
            P(),
            P(),
            P(),
            P(),
        ),
        out_specs=P("rows", "cols", None),
        check_vma=False,
    )
```

time: 784 us -> 258 us (0.33)
  waiting for transfers between devices: 320 us -> 0 us
  Pallas kernels: 0 us -> 253 us
  blocking collectives: 174 us -> 0 us
  local copies, waits for them, and re-layouts: 151 us -> 4.9 us
  matrix products: 101 us -> 0 us
  other arithmetic: 19.3 us -> 0 us
  starting transfers between devices: 11.5 us -> 0 us
    all_to_all x2 -> x0, waiting for transfers between devices: 320 us -> none  [the longest x1 183 us: on_device(): lax.all_to_all(lax.all_to_all(spread, 'rows', split_axis=1, concat_axis=3...]
    pallas_call x0 -> x3, Pallas kernels: none -> 253 us  [the longest x1 235 us: on_device(): pl.pallas_call(functools.partial(window_kernel, row_count, col_count, win...]
    all_to_all x2 -> x0, blocking collectives: 174 us -> none  [the longest x1 100 us: on_device(): lax.all_to_all(spread, 'rows', split_axis=1, concat_axis=3, tiled=True)]
    dot_general x36 -> x0, matrix products: 72.4 us -> none  [the longest x8 29.8 us: window_grads(): jnp.einsum('hqk,qhd->khd', attention.astype(jnp.bfloat16), grad_heads, pr...]
    all_to_all x7 -> x0, local copies, waits for them, and re-layouts: 48.8 us -> none  [the longest x2 18 us: on_device(): lax.all_to_all(spread, 'rows', split_axis=1, concat_axis=3, tiled=True)]
    dynamic_slice x64 -> x0, local copies, waits for them, and re-layouts: 36.1 us -> none  [on_device(): lax.map(window_grads, (grouped[0], grouped[1], grouped[2], grouped[3]))]
    sub x8 -> x0, matrix products: 28.3 us -> none  [window_grads(): attention = jax.nn.softmax(scores, axis=-1)]
    dynamic_update_slice x40 -> x0, local copies, waits for them, and re-layouts: 23.7 us -> none  [on_device(): lax.map(window_grads, (grouped[0], grouped[1], grouped[2], grouped[3]))]
  transfers between devices with their start and end apart: 2 -> 0, of which waited for: 2 -> 0; matrix products, arithmetic and copies ran while one was open for 0% -> 0% of each run, Pallas kernels for 0% -> 0%
where the time goes in v1:
time: 258 us
  Pallas kernels  253 us (98%)
  local copies, waits for them, and re-layouts  4.9 us (2%)
    pallas_call x1, Pallas kernels, on_device(): pl.pallas_call(functools.partial(window_kernel, row_count, col_count, win...  235 us
    pallas_call x1, Pallas kernels, on_device(): pl.pallas_call(pack_kernel, grid=(row_count,), in_specs=[perm_spec, weigh...  10.2 us
    pallas_call x1, Pallas kernels, on_device(): pl.pallas_call(norm_kernel, grid=(row_count,), in_specs=[perm_spec, pl.Bl...  7.88 us

profile of v1, /device:TPU:0, one launch (start us, length us, event | category | flops | bytes accessed | tf_op | source)
XLA Modules:
  0.0 257.9 jit_solution(9671077018436204111)
XLA Ops:
  0.0 0.0 copy-start.1
  0.0 1.6 copy-done.1
  1.6 0.0 copy-start.3
  1.6 1.0 copy-done.3
  2.6 0.0 copy-start.7
  2.6 0.9 copy-done.7
  3.5 0.0 copy-start.4
  3.5 0.0 copy-start.5
  3.5 0.0 copy-start.6
  3.5 10.2 %shard_map.118 = bf16[4,8,4,4,16,512]{5,4,3,2,1,0:T(8,128)(2,1)} custom-call(bf16[256,256]{1,0:T(8,128)(2,1)S(1)} %copy-done.7, bf16[512,512]{1,0:T(8,128)(2,1)S(1)} %copy-done.3, bf16[2,16,64,512]{3,2,1,0:T(8,128)(2,1)S(1)} %bitcast.9, bf16[2,16,64,512]{3,2,1,0:T(8,128)(2,1)} %bitcast.14, bf16[2,16,64,512]{3,2,1,0:T(8,128)(2,1)} %bitcast.15, ...), custom_call_target="tpu_custom_call" | custom-call | tf_op jit(solution)/shard_map/pallas_call | solution.py:224
  13.8 0.0 copy-done.4
  13.8 0.0 copy-done.5
  13.8 0.0 copy-done.6
  13.8 0.0 copy-start.9
  13.8 0.0 copy-start.2
  13.8 0.0 copy-start.8
  13.8 234.8 %shard_map.119 = bf16[4,32,16,512]{3,2,1,0:T(8,128)(2,1)S(1)} custom-call(bf16[4,32,4,16,512]{4,3,2,1,0:T(8,128)(2,1)} %bitcast.11, bf16[512,512]{1,0:T(8,128)(2,1)S(1)} %copy-done.4, bf16[512,512]{1,0:T(8,128)(2,1)S(1)} %copy-done.5, bf16[512,512]{1,0:T(8,128)(2,1)S(1)} %copy-done.6), custom_call_target="tpu_custom_call" | custom-call | tf_op jit(solution)/shard_map/pallas_call | solution.py:238
  248.6 0.0 copy-start
  248.7 1.3 copy-done
  250.0 0.0 copy-done.9
  250.0 0.0 copy-done.2
  250.0 0.0 copy-done.8
  250.0 7.9 %shard_map.120 = f32[2,16,64,512]{3,2,1,0:T(8,128)} custom-call(bf16[256,256]{1,0:T(8,128)(2,1)S(1)} %copy-done.8, bf16[1,512]{1,0:T(2,128)(2,1)S(1)} %reshape.28.gain_ref, bf16[2,16,64,512]{3,2,1,0:T(8,128)(2,1)S(1)} %bitcast.10, bf16[2,16,64,512]{3,2,1,0:T(8,128)(2,1)} %bitcast.13, bf16[4,8,4,16,512]{4,3,2,1,0:T(8,128)(2,1)} %bitcast.8), custom_call_target="tpu_custom_call" | custom-call | tf_op jit(solution)/shard_map/pallas_call | solution.py:264
  (1 shorter events, 0.0 us)
Async XLA Ops:
  0.0 1.6 copy-start.1
  1.6 1.0 copy-start.3
  2.6 0.9 copy-start.7
  3.5 10.2 %copy-start.4 = (bf16[512,512]{1,0:T(8,128)(2,1)S(1)}, bf16[512,512]{1,0:T(8,128)(2,1)}, u32[]{:S(2)}) copy-start(bf16[512,512]{1,0:T(8,128)(2,1)} %w_query_ref.1) | copy-start | bytes 1572868
  3.5 10.2 %copy-start.5 = (bf16[512,512]{1,0:T(8,128)(2,1)S(1)}, bf16[512,512]{1,0:T(8,128)(2,1)}, u32[]{:S(2)}) copy-start(bf16[512,512]{1,0:T(8,128)(2,1)} %w_key_ref.1) | copy-start | bytes 1572868
  3.5 10.2 %copy-start.6 = (bf16[512,512]{1,0:T(8,128)(2,1)S(1)}, bf16[512,512]{1,0:T(8,128)(2,1)}, u32[]{:S(2)}) copy-start(bf16[512,512]{1,0:T(8,128)(2,1)} %w_value_ref.1) | copy-start | bytes 1572868
  13.8 236.2 %copy-start.9 = (bf16[512]{0:T(512)(128)(2,1)S(1)}, bf16[512]{0:T(512)(128)(2,1)}, u32[]{:S(2)}) copy-start(bf16[512]{0:T(512)(128)(2,1)} %param.13) | copy-start | bytes 3076
  13.8 236.2 %copy-start.2 = (bf16[32,64,512]{2,1,0:T(8,128)(2,1)S(1)}, bf16[32,64,512]{2,1,0:T(8,128)(2,1)}, u32[]{:S(2)}) copy-start(bf16[32,64,512]{2,1,0:T(8,128)(2,1)} %param.12) | copy-start | bytes 6291460
  13.8 236.2 %copy-start.8 = (bf16[256,256]{1,0:T(8,128)(2,1)S(1)}, bf16[256,256]{1,0:T(8,128)(2,1)}, u32[]{:S(2)}) copy-start(bf16[256,256]{1,0:T(8,128)(2,1)} %constant.5.clone.perm_ref) | copy-start | bytes 393220
  248.6 1.3 copy-start

commit v2 on v1

--- a/solution.py
+++ b/solution.py
@@ -18,6 +18,7 @@
 EXP2_FACTOR = FACTOR * float(np.log2(np.e))
 MESH = pl.DeviceIdType.MESH
 VMEM_BYTES = 50 * 1024 * 1024
+WINDOW_VMEM_BYTES = 60 * 1024 * 1024
 F32 = jnp.float32
 BF16 = jnp.bfloat16
 
@@ -28,17 +29,6 @@
 
 def dot_t(left, right):
     return lax.dot_general(left, right, (((1,), (1,)), ((), ())), preferred_element_type=F32)
-
-
-def pack_kernel(perm_ref, w_out_ref, q_ref, k_ref, v_ref, g_ref, out_ref):
-    chunks, _, cols, _, rows, _ = out_ref.shape
-    perm = perm_ref[...]
-    tokens = perm.shape[0]
-    for member, ref in enumerate((q_ref, k_ref, v_ref, g_ref)):
-        ordered = dot(perm, ref[...].reshape(tokens, D)).astype(BF16)
-        if member == 3:
-            ordered = dot_t(ordered, w_out_ref[...]).astype(BF16)
-        out_ref[:, 0, :, member] = ordered.reshape(chunks, cols, rows, D)
 
 
 def norm_kernel(perm_ref, gain_ref, x_ref, g_ref, back_ref, out_ref):
@@ -60,12 +50,19 @@
 
 
 def window_kernel(
-    row_count, col_count, wins, part,
-    send_ref, w_query_ref, w_key_ref, w_value_ref, back_ref,
-    recv, reply, q_win, k_win, v_win, g_win, k_turned, dq_turned, dk_win, dv_win,
-    send_sem, recv_sem, reply_sem, back_sem,
+    row_count, col_count, wins, part, col_part,
+    q_ref, k_ref, v_ref, g_ref, w_query_ref, w_key_ref, w_value_ref, w_out_ref, back_ref,
+    stage, packed, recv, reply, weights_in, perm,
+    q_win, k_win, v_win, g_win, k_turned, dq_turned, dk_win, dv_win,
+    stage_sem, weight_sem, send_sem, recv_sem, reply_sem, back_sem,
 ):
-    chunks, devices, _, rows, _ = send_ref.shape
+    chunks, devices, _, rows, _ = packed.shape
+    _, _, row_reps, phase_part, cols_dev, _ = stage.shape
+    row_part = q_ref.shape[1] // row_count
+    phases = row_part // phase_part
+    phase_chunks = chunks // phases
+    tokens = row_reps * phase_part * cols_dev
+    steps = phases * row_count
     my_row, my_col = lax.axis_index("rows"), lax.axis_index("cols")
     me = my_row * col_count + my_col
 
@@ -74,26 +71,32 @@
         col = lax.rem(my_col + lax.rem(step, col_count), col_count)
         return row, col, row * col_count + col
 
-    barrier = pltpu.get_barrier_semaphore()
-
-    @pl.loop(1, devices)
-    def _(step):
-        row, col, _ = peer_of(step)
-        pl.semaphore_signal(barrier, inc=1, device_id=(row, col), device_id_type=MESH)
-
-    pl.semaphore_wait(barrier, devices - 1)
-
-    @pl.loop(0, chunks)
-    def _(chunk):
-        pltpu.make_async_copy(
-            send_ref.at[chunk, me], recv.at[chunk, me], recv_sem.at[chunk]
-        ).start()
-
-        @pl.loop(1, devices)
-        def _(step):
-            row, col, index = peer_of(step)
+    def row_of(step):
+        return lax.rem(my_row + 1 + step, row_count)
+
+    def stage_copies(step):
+        slot = lax.rem(step, 2)
+        first = row_of(step) * row_part + (step // row_count) * phase_part
+        return [
+            pltpu.make_async_copy(
+                ref.at[:, pl.ds(first, phase_part)], stage.at[slot, member], stage_sem.at[slot, member]
+            )
+            for member, ref in enumerate((q_ref, k_ref, v_ref, g_ref))
+        ]
+
+    def send(chunk, row, col):
+        index = row * col_count + col
+
+        @pl.when(index == me)
+        def _():
+            pltpu.make_async_copy(
+                packed.at[chunk, me], recv.at[chunk, me], recv_sem.at[chunk]
+            ).start()
+
+        @pl.when(index != me)
+        def _():
             pltpu.make_async_remote_copy(
-                src_ref=send_ref.at[chunk, index],
+                src_ref=packed.at[chunk, index],
                 dst_ref=recv.at[chunk, me],
                 send_sem=send_sem.at[chunk],
                 recv_sem=recv_sem.at[chunk],
@@ -101,6 +104,64 @@
                 device_id_type=MESH,
             ).start()
 
+    weight_copies = [
+        pltpu.make_async_copy(ref, weights_in.at[member], weight_sem.at[member])
+        for member, ref in enumerate((w_out_ref, w_query_ref, w_key_ref, w_value_ref))
+    ]
+    for copy in stage_copies(0) + weight_copies:
+        copy.start()
+    barrier = pltpu.get_barrier_semaphore()
+
+    @pl.loop(1, devices)
+    def _(step):
+        row, col, _ = peer_of(step)
+        pl.semaphore_signal(barrier, inc=1, device_id=(row, col), device_id_type=MESH)
+
+    target = lax.broadcasted_iota(jnp.int32, (tokens, tokens), 0)
+    source = lax.broadcasted_iota(jnp.int32, (tokens, tokens), 1)
+    col_reps = part // row_reps
+    chunk_in, col_in = target // (col_count * rows), target // rows % col_count
+    window = chunk_in * wins + target % rows // part
+    row_rep, col_rep = target % part // col_reps, target % col_reps
+    wanted = (row_rep * phase_part + window // col_part) * col_reps + col_rep
+    wanted = (wanted * col_count + col_in) * col_part + window % col_part
+    perm[...] = (source == wanted).astype(BF16)
+    weight_copies[0].wait()
+    pl.semaphore_wait(barrier, devices - 1)
+
+    @pl.loop(0, steps)
+    def _(step):
+        @pl.when(step + 1 < steps)
+        def _():
+            for copy in stage_copies(step + 1):
+                copy.start()
+
+        for copy in stage_copies(step):
+            copy.wait()
+        slot, phase, row = lax.rem(step, 2), step // row_count, row_of(step)
+        for member in range(4):
+            ordered = dot(perm[...], stage[slot, member].reshape(tokens, D)).astype(BF16)
+            if member == 3:
+                ordered = dot_t(ordered, weights_in[0]).astype(BF16)
+            packed[
+                pl.ds(phase * phase_chunks, phase_chunks), pl.ds(row * col_count, col_count), member
+            ] = ordered.reshape(phase_chunks, col_count, rows, D)
+
+        @pl.when(phase == 0)
+        def _():
+            @pl.loop(0, col_count)
+            def _(shift):
+                send(0, row, lax.rem(my_col + 1 + shift, col_count))
+
+    @pl.loop(1, chunks)
+    def _(chunk):
+        @pl.loop(0, devices)
+        def _(step):
+            row, col, _ = peer_of(step)
+            send(chunk, row, col)
+
+    for copy in weight_copies[1:]:
+        copy.wait()
     lane_head = lax.broadcasted_iota(jnp.int32, (1, LANES), 1) // HEAD_DIM
     spread = devices * rows
 
@@ -142,9 +203,9 @@
                 dv_win[:, lanes] = value_grad.astype(BF16)
                 dk_win[:, lanes] = (key_grad * FACTOR).astype(BF16)
 
-            total = dot_t(dq_turned[...].T.astype(BF16), w_query_ref[...])
-            total += dot_t(dk_win[...], w_key_ref[...])
-            total += dot_t(dv_win[...], w_value_ref[...])
+            total = dot_t(dq_turned[...].T.astype(BF16), weights_in[1])
+            total += dot_t(dk_win[...], weights_in[2])
+            total += dot_t(dv_win[...], weights_in[3])
             place_t = lax.broadcasted_iota(jnp.int32, (spread, LENGTH), 0)
             slot_t = lax.broadcasted_iota(jnp.int32, (spread, LENGTH), 1)
             put = (place_t == (slot_t // part) * rows + win * part + slot_t % part).astype(BF16)
@@ -169,7 +230,7 @@
 
     @pl.loop(0, chunks)
     def _(chunk):
-        sent = send_ref.at[chunk, pl.ds(0, devices - 1)]
+        sent = packed.at[chunk, pl.ds(0, devices - 1)]
         pltpu.make_async_copy(sent, sent, send_sem.at[chunk]).wait()
         replied = reply.at[chunk, pl.ds(0, devices - 1)]
         pltpu.make_async_copy(replied, replied, reply_sem.at[chunk]).wait()
@@ -200,6 +261,8 @@
     wins = next(n for n in range(1, windows + 1) if windows % n == 0 and n * part % 16 == 0)
     chunks, rows = windows // wins, wins * part
 
+    phase_part = max(1, wins // col_part)
+    phase_tokens = row_reps * phase_part * cols_dev
     tokens = row_reps * row_part * cols_dev
     order = (
         np.arange(tokens)
@@ -211,38 +274,29 @@
     )
     perm = np.zeros((tokens, tokens), np.float32)
     perm[np.arange(tokens), order] = 1.0
-    forward, backward = jnp.asarray(perm, BF16), jnp.asarray(perm.T, BF16)
+    backward = jnp.asarray(perm.T, BF16)
 
     def blocks(array):
         return array.reshape(row_reps, row_stride, cols_dev, D)
 
     token_spec = pl.BlockSpec((row_reps, row_part, cols_dev, D), lambda r: (0, r, 0, 0))
     perm_spec = pl.BlockSpec((tokens, tokens), lambda r: (0, 0))
-    weight_spec = pl.BlockSpec((D, D), lambda r: (0, 0))
     params = pltpu.CompilerParams(vmem_limit_bytes=VMEM_BYTES)
 
-    packed = pl.pallas_call(
-        pack_kernel,
-        grid=(row_count,),
-        in_specs=[perm_spec, weight_spec] + [token_spec] * 4,
-        out_specs=pl.BlockSpec(
-            (chunks, 1, col_count, 4, rows, D), lambda r: (0, r, 0, 0, 0, 0)
-        ),
-        out_shape=jax.ShapeDtypeStruct((chunks, row_count, col_count, 4, rows, D), BF16),
-        compiler_params=params,
-    )(forward, w_out, blocks(saved_queries), blocks(saved_keys), blocks(saved_values), blocks(out_grad))
-
-    vmem = pl.BlockSpec(memory_space=pltpu.VMEM)
     hbm = pl.BlockSpec(memory_space=pl.ANY)
     window = pltpu.VMEM((LENGTH, D), BF16)
     back = pl.pallas_call(
-        functools.partial(window_kernel, row_count, col_count, wins, part),
-        in_specs=[hbm, vmem, vmem, vmem],
+        functools.partial(window_kernel, row_count, col_count, wins, part, col_part),
+        in_specs=[hbm] * 8,
         out_specs=hbm,
         out_shape=jax.ShapeDtypeStruct((chunks, devices, rows, D), BF16),
         scratch_shapes=[
+            pltpu.VMEM((2, 4, row_reps, phase_part, cols_dev, D), BF16),
+            pltpu.VMEM((chunks, devices, 4, rows, D), BF16),
             pltpu.VMEM((chunks, devices, 4, rows, D), BF16),
             pltpu.VMEM((chunks, devices, rows, D), BF16),
+            pltpu.VMEM((4, D, D), BF16),
+            pltpu.VMEM((phase_tokens, phase_tokens), BF16),
             window,
             window,
             window,
@@ -251,15 +305,20 @@
             pltpu.VMEM((D, LENGTH), F32),
             window,
             window,
+            pltpu.SemaphoreType.DMA((2, 4)),
+            pltpu.SemaphoreType.DMA((4,)),
             pltpu.SemaphoreType.DMA((chunks,)),
             pltpu.SemaphoreType.DMA((chunks,)),
             pltpu.SemaphoreType.DMA((chunks,)),
             pltpu.SemaphoreType.DMA((chunks,)),
         ],
         compiler_params=pltpu.CompilerParams(
-            collective_id=0, has_side_effects=True, vmem_limit_bytes=VMEM_BYTES
+            collective_id=0, has_side_effects=True, vmem_limit_bytes=WINDOW_VMEM_BYTES
         ),
-    )(packed.reshape(chunks, devices, 4, rows, D), w_query, w_key, w_value)
+    )(
+        blocks(saved_queries), blocks(saved_keys), blocks(saved_values), blocks(out_grad),
+        w_query, w_key, w_value, w_out,
+    )
 
     result = pl.pallas_call(
         norm_kernel,

time: 258 us -> 245 us (0.950)
  Pallas kernels: 253 us -> 244 us
  local copies, waits for them, and re-layouts: 4.9 us -> 0.69 us
    pallas_call x1 -> x0, Pallas kernels: 10.2 us -> none  [on_device(): pl.pallas_call(pack_kernel, grid=(row_count,), in_specs=[perm_spec, weigh...]
    unnamed x20 -> x4, local copies, waits for them, and re-layouts: 4.9 us -> 0.01 us
where the time goes in v2:
time: 245 us; the launch traced here: 244 us
  Pallas kernels  244 us (100%)
    pallas_call x1, Pallas kernels, on_device(): pl.pallas_call(functools.partial(window_kernel, row_count, col_count, win...  236 us
    pallas_call x1, Pallas kernels, on_device(): pl.pallas_call(norm_kernel, grid=(row_count,), in_specs=[perm_spec, pl.Bl...  7.88 us

profile of v2, /device:TPU:0, one launch (start us, length us, event | category | flops | bytes accessed | tf_op | source)
XLA Modules:
  0.0 244.2 jit_solution(3949136025747870493)
XLA Ops:
  0.0 0.7 reshape.25.gain_ref
  0.7 0.0 copy-start
  0.7 0.0 copy-start.1
  0.7 235.6 %shard_map.109 = bf16[4,32,16,512]{3,2,1,0:T(8,128)(2,1)} custom-call(bf16[2,16,64,512]{3,2,1,0:T(8,128)(2,1)} %bitcast.11, bf16[2,16,64,512]{3,2,1,0:T(8,128)(2,1)} %bitcast.12, bf16[2,16,64,512]{3,2,1,0:T(8,128)(2,1)} %bitcast.13, bf16[2,16,64,512]{3,2,1,0:T(8,128)(2,1)} %bitcast.8, bf16[512,512]{1,0:T(8,128)(2,1)} %w_query_ref.1, ...), custom_call_target="tpu_custom_call" | custom-call | tf_op jit(solution)/shard_map/pallas_call | solution.py:288
  236.3 0.0 copy-done
  236.3 0.0 copy-done.1
  236.3 7.9 %shard_map.110 = f32[2,16,64,512]{3,2,1,0:T(8,128)} custom-call(bf16[256,256]{1,0:T(8,128)(2,1)S(1)} %copy-done.1, bf16[1,512]{1,0:T(2,128)(2,1)S(1)} %reshape.25.gain_ref, bf16[2,16,64,512]{3,2,1,0:T(8,128)(2,1)S(1)} %bitcast.7, bf16[2,16,64,512]{3,2,1,0:T(8,128)(2,1)} %bitcast.9, bf16[4,8,4,16,512]{4,3,2,1,0:T(8,128)(2,1)} %bitcast.10), custom_call_target="tpu_custom_call" | custom-call | tf_op jit(solution)/shard_map/pallas_call | solution.py:323
Async XLA Ops:
  0.7 235.6 %copy-start = (bf16[32,64,512]{2,1,0:T(8,128)(2,1)S(1)}, bf16[32,64,512]{2,1,0:T(8,128)(2,1)}, u32[]{:S(2)}) copy-start(bf16[32,64,512]{2,1,0:T(8,128)(2,1)} %param.11) | copy-start | bytes 6291460
  0.7 235.6 %copy-start.1 = (bf16[256,256]{1,0:T(8,128)(2,1)S(1)}, bf16[256,256]{1,0:T(8,128)(2,1)}, u32[]{:S(2)}) copy-start(bf16[256,256]{1,0:T(8,128)(2,1)} %constant.2.clone.perm_ref) | copy-start | bytes 393220

commit v3 on v2

--- a/solution.py
+++ b/solution.py
@@ -1,4 +1,5 @@
 import functools
+import math
 
 import jax
 import jax.numpy as jnp
@@ -34,19 +35,25 @@
 def norm_kernel(perm_ref, gain_ref, x_ref, g_ref, back_ref, out_ref):
     perm = perm_ref[...]
     tokens = perm.shape[0]
-    input_grad = dot(perm, back_ref[...].reshape(tokens, D))
-    values_in = x_ref[...].reshape(tokens, D).astype(F32)
-    centred = values_in - jnp.mean(values_in, axis=-1, keepdims=True)
-    variance = jnp.mean(centred * centred, axis=-1, keepdims=True)
-    inv_std = lax.rsqrt(variance + 1e-05)
-    normed = centred * inv_std
-    scaled = input_grad * gain_ref[...].astype(F32)
-    branch = inv_std * (
-        scaled
-        - jnp.mean(scaled, axis=-1, keepdims=True)
-        - normed * jnp.mean(scaled * normed, axis=-1, keepdims=True)
-    )
-    out_ref[...] = (g_ref[...].reshape(tokens, D).astype(F32) + branch).reshape(out_ref.shape)
+    gain = gain_ref[...].astype(F32).reshape(1, D)
+    fold = back_ref.shape[1]
+    part = x_ref.shape[1] // fold
+    for index in range(fold):
+        span = slice(index * part, (index + 1) * part)
+        input_grad = dot(perm, back_ref[:, index].reshape(tokens, D))
+        values_in = x_ref[:, span].reshape(tokens, D).astype(F32)
+        centred = values_in - jnp.mean(values_in, axis=-1, keepdims=True)
+        variance = jnp.mean(centred * centred, axis=-1, keepdims=True)
+        inv_std = lax.rsqrt(variance + 1e-05)
+        normed = centred * inv_std
+        scaled = input_grad * gain
+        branch = inv_std * (
+            scaled
+            - jnp.mean(scaled, axis=-1, keepdims=True)
+            - normed * jnp.mean(scaled * normed, axis=-1, keepdims=True)
+        )
+        total = g_ref[:, span].reshape(tokens, D).astype(F32) + branch
+        out_ref[:, span] = total.reshape(x_ref.shape[0], part, x_ref.shape[2], D)
 
 
 def window_kernel(
@@ -279,7 +286,8 @@
     def blocks(array):
         return array.reshape(row_reps, row_stride, cols_dev, D)
 
-    token_spec = pl.BlockSpec((row_reps, row_part, cols_dev, D), lambda r: (0, r, 0, 0))
+    fold = math.gcd(row_count, 2)
+    token_spec = pl.BlockSpec((row_reps, fold * row_part, cols_dev, D), lambda r: (0, r, 0, 0))
     perm_spec = pl.BlockSpec((tokens, tokens), lambda r: (0, 0))
     params = pltpu.CompilerParams(vmem_limit_bytes=VMEM_BYTES)
 
@@ -322,20 +330,20 @@
 
     result = pl.pallas_call(
         norm_kernel,
-        grid=(row_count,),
+        grid=(row_count // fold,),
         in_specs=[
             perm_spec,
-            pl.BlockSpec((1, D), lambda r: (0, 0)),
+            pl.BlockSpec((D,), lambda r: (0,)),
             token_spec,
             token_spec,
-            pl.BlockSpec((chunks, 1, col_count, rows, D), lambda r: (0, r, 0, 0, 0)),
+            pl.BlockSpec((chunks, fold, col_count, rows, D), lambda r: (0, r, 0, 0, 0)),
         ],
         out_specs=token_spec,
         out_shape=jax.ShapeDtypeStruct((row_reps, row_stride, cols_dev, D), F32),
         compiler_params=params,
     )(
         backward,
-        norm_gain.reshape(1, D),
+        norm_gain,
         blocks(block_input),
         blocks(out_grad),
         back.reshape(chunks, row_count, col_count, rows, D),

time: 245 us -> 242 us (0.988)
  no operation moved by 1% of the time
where the time goes in v3:
time: 242 us
  Pallas kernels  242 us (100%)
    pallas_call x1, Pallas kernels, on_device(): pl.pallas_call(functools.partial(window_kernel, row_count, col_count, win...  236 us
    pallas_call x1, Pallas kernels, on_device(): pl.pallas_call(norm_kernel, grid=(row_count // fold,), in_specs=[perm_spe...  6.28 us

profile of v3, /device:TPU:0, one launch (start us, length us, event | category | flops | bytes accessed | tf_op | source)
XLA Modules:
  0.0 242.0 jit_solution(7843147531788991762)
XLA Ops:
  0.0 0.0 copy-start
  0.0 0.0 copy-start.1
  0.0 0.0 copy-start.2
  0.0 235.7 %shard_map.109 = bf16[4,32,16,512]{3,2,1,0:T(8,128)(2,1)} custom-call(bf16[2,16,64,512]{3,2,1,0:T(8,128)(2,1)} %bitcast.11, bf16[2,16,64,512]{3,2,1,0:T(8,128)(2,1)} %bitcast.12, bf16[2,16,64,512]{3,2,1,0:T(8,128)(2,1)} %bitcast.13, bf16[2,16,64,512]{3,2,1,0:T(8,128)(2,1)} %bitcast.8, bf16[512,512]{1,0:T(8,128)(2,1)} %w_query_ref.1, ...), custom_call_target="tpu_custom_call" | custom-call | tf_op jit(solution)/shard_map/pallas_call | solution.py:296
  235.7 0.0 copy-done
  235.7 0.0 copy-done.1
  235.7 0.0 copy-done.2
  235.7 6.3 %shard_map.110 = f32[2,16,64,512]{3,2,1,0:T(8,128)} custom-call(bf16[256,256]{1,0:T(8,128)(2,1)S(1)} %copy-done.1, bf16[512]{0:T(512)(128)(2,1)S(1)} %copy-done.2, bf16[2,16,64,512]{3,2,1,0:T(8,128)(2,1)S(1)} %bitcast.7, bf16[2,16,64,512]{3,2,1,0:T(8,128)(2,1)} %bitcast.9, bf16[4,8,4,16,512]{4,3,2,1,0:T(8,128)(2,1)} %bitcast.10), custom_call_target="tpu_custom_call" | custom-call | tf_op jit(solution)/shard_map/pallas_call | solution.py:331
Async XLA Ops:
  0.0 235.7 %copy-start = (bf16[32,64,512]{2,1,0:T(8,128)(2,1)S(1)}, bf16[32,64,512]{2,1,0:T(8,128)(2,1)}, u32[]{:S(2)}) copy-start(bf16[32,64,512]{2,1,0:T(8,128)(2,1)} %param.11) | copy-start | bytes 6291460
  0.0 235.7 %copy-start.1 = (bf16[256,256]{1,0:T(8,128)(2,1)S(1)}, bf16[256,256]{1,0:T(8,128)(2,1)}, u32[]{:S(2)}) copy-start(bf16[256,256]{1,0:T(8,128)(2,1)} %constant.2.clone.perm_ref) | copy-start | bytes 393220
  0.0 235.7 %copy-start.2 = (bf16[512]{0:T(512)(128)(2,1)S(1)}, bf16[512]{0:T(512)(128)(2,1)}, u32[]{:S(2)}) copy-start(bf16[512]{0:T(512)(128)(2,1)} %gain_ref.1) | copy-start | bytes 3076

commit v4 on v3

--- a/solution.py
+++ b/solution.py
@@ -45,13 +45,9 @@
         centred = values_in - jnp.mean(values_in, axis=-1, keepdims=True)
         variance = jnp.mean(centred * centred, axis=-1, keepdims=True)
         inv_std = lax.rsqrt(variance + 1e-05)
-        normed = centred * inv_std
         scaled = input_grad * gain
-        branch = inv_std * (
-            scaled
-            - jnp.mean(scaled, axis=-1, keepdims=True)
-            - normed * jnp.mean(scaled * normed, axis=-1, keepdims=True)
-        )
+        slope = inv_std * inv_std * jnp.mean(scaled * centred, axis=-1, keepdims=True)
+        branch = inv_std * (scaled - jnp.mean(scaled, axis=-1, keepdims=True) - centred * slope)
         total = g_ref[:, span].reshape(tokens, D).astype(F32) + branch
         out_ref[:, span] = total.reshape(x_ref.shape[0], part, x_ref.shape[2], D)
 
@@ -286,7 +282,7 @@
     def blocks(array):
         return array.reshape(row_reps, row_stride, cols_dev, D)
 
-    fold = math.gcd(row_count, 2)
+    fold = math.gcd(row_count, 4)
     token_spec = pl.BlockSpec((row_reps, fold * row_part, cols_dev, D), lambda r: (0, r, 0, 0))
     perm_spec = pl.BlockSpec((tokens, tokens), lambda r: (0, 0))
     params = pltpu.CompilerParams(vmem_limit_bytes=VMEM_BYTES)

time: 242 us -> 242 us (level)
  no operation moved by 1% of the time
where the time goes in v4:
time: 242 us
  Pallas kernels  242 us (100%)
    pallas_call x1, Pallas kernels, on_device(): pl.pallas_call(functools.partial(window_kernel, row_count, col_count, win...  236 us
    pallas_call x1, Pallas kernels, on_device(): pl.pallas_call(norm_kernel, grid=(row_count // fold,), in_specs=[perm_spe...  5.84 us

profile of v4, /device:TPU:0, one launch (start us, length us, event | category | flops | bytes accessed | tf_op | source)
XLA Modules:
  0.0 241.6 jit_solution(7278800310527727725)
XLA Ops:
  0.0 0.0 copy-start
  0.0 0.0 copy-start.1
  0.0 0.0 copy-start.2
  0.0 235.7 %shard_map.109 = bf16[4,32,16,512]{3,2,1,0:T(8,128)(2,1)} custom-call(bf16[2,16,64,512]{3,2,1,0:T(8,128)(2,1)} %bitcast.11, bf16[2,16,64,512]{3,2,1,0:T(8,128)(2,1)} %bitcast.12, bf16[2,16,64,512]{3,2,1,0:T(8,128)(2,1)} %bitcast.13, bf16[2,16,64,512]{3,2,1,0:T(8,128)(2,1)} %bitcast.8, bf16[512,512]{1,0:T(8,128)(2,1)} %w_query_ref.1, ...), custom_call_target="tpu_custom_call" | custom-call | tf_op jit(solution)/shard_map/pallas_call | solution.py:292
  235.7 0.0 copy-done
  235.7 0.0 copy-done.1
  235.7 0.0 copy-done.2
  235.7 5.8 %shard_map.110 = f32[2,16,64,512]{3,2,1,0:T(8,128)} custom-call(bf16[256,256]{1,0:T(8,128)(2,1)S(1)} %copy-done.1, bf16[512]{0:T(512)(128)(2,1)S(1)} %copy-done.2, bf16[2,16,64,512]{3,2,1,0:T(8,128)(2,1)S(1)} %bitcast.7, bf16[2,16,64,512]{3,2,1,0:T(8,128)(2,1)} %bitcast.9, bf16[4,8,4,16,512]{4,3,2,1,0:T(8,128)(2,1)} %bitcast.10), custom_call_target="tpu_custom_call" | custom-call | tf_op jit(solution)/shard_map/pallas_call | solution.py:327
Async XLA Ops:
  0.0 235.7 %copy-start = (bf16[32,64,512]{2,1,0:T(8,128)(2,1)S(1)}, bf16[32,64,512]{2,1,0:T(8,128)(2,1)}, u32[]{:S(2)}) copy-start(bf16[32,64,512]{2,1,0:T(8,128)(2,1)} %param.11) | copy-start | bytes 6291460
  0.0 235.7 %copy-start.1 = (bf16[256,256]{1,0:T(8,128)(2,1)S(1)}, bf16[256,256]{1,0:T(8,128)(2,1)}, u32[]{:S(2)}) copy-start(bf16[256,256]{1,0:T(8,128)(2,1)} %constant.2.clone.perm_ref) | copy-start | bytes 393220
  0.0 235.7 %copy-start.2 = (bf16[512]{0:T(512)(128)(2,1)S(1)}, bf16[512]{0:T(512)(128)(2,1)}, u32[]{:S(2)}) copy-start(bf16[512]{0:T(512)(128)(2,1)} %gain_ref.1) | copy-start | bytes 3076
